TPU v7x, 256 devices: a whole 4x4x8 slice. The times are simulated.
256 devices in a mesh: section: 2 (over y_hi), dp: 8 (over x, core), tensor: 16 (over y_lo, z).
Axes of the slice: x: 4, y: 4 (y_hi: 2, y_lo: 2; y = y_hi * 2 + y_lo), z: 8, core: 2. Of those that a mesh axis runs over, the one named last changes fastest.
Arguments:
- activations: bfloat16 [2, 8, 256, 3584], P(None, 'dp', 'tensor'), may hold values from -24 to 24
- norm_gain: bfloat16 [2, 3584], P('section'), may hold values from 0.099609375 to 1.8984375
- query_matrix: bfloat16 [2, 3584, 4096], P('section', None, 'tensor'), may hold values from -0.09375 to 0.09375
- key_weight: bfloat16 [2, 3584, 4096], P('section', None, 'tensor'), may hold values from -0.09375 to 0.09375
- value_weight: bfloat16 [2, 3584, 8192], P('section', None, 'tensor'), may hold values from -0.09375 to 0.09375
- decay_down: bfloat16 [2, 3584, 16], P('section'), may hold values from -0.09375 to 0.09375
- decay_up: bfloat16 [2, 16, 4096], P('section', None, 'tensor'), may hold values from -1.5 to 1.5
- decay_bias: float32 [2, 4096], P('section', 'tensor'), may hold values from -3 to 5
- head_gain: bfloat16 [2, 8192], P('section', 'tensor'), may hold values from 0.099609375 to 1.8984375
- output_matrix: bfloat16 [2, 8192, 3584], P('section', 'tensor'), may hold values from -0.0625 to 0.0625
Outputs:
- finals: bfloat16 [2, 8, 256, 3584], P('section', 'dp', 'tensor')
All inputs are finite; a program needn't handle non-finite values.
Results may differ from a plain program's by a relative error of at most 0.029.
Values may be sent and summed in bfloat16 or wider, within the bound.
No kernel may reach another device: no remote copies, remote signals or barrier semaphores. Data moves between devices by JAX's collectives and lax.ppermute only.
A program may use at most 64 MiB of HBM per device.

v0:
```python
import jax
import jax.numpy as jnp
from jax import lax
from jax.sharding import PartitionSpec as P

KEY = 64
VAL = 128
SPAN = 64


HIGH = lax.Precision.HIGHEST


def shifted(value, axis, steps):
    count = lax.axis_size(axis)
    leading, last = (max(0, -steps), min(count, count - steps))
    return lax.ppermute(value, axis, [(source, source + steps) for source in range(leading, last)])


def normalize(values, gain):
    return values * lax.rsqrt(jnp.mean(values * values, axis=-1, keepdims=True) + 1e-05) * gain


def head_normalize(values, gain):
    return (
        values
        * lax.rsqrt(jnp.maximum(jnp.mean(values * values, axis=-1, keepdims=True), 1.0))
        * gain
    )


def blockwise(query, keys, values, decay_logarithm):
    seq_count, length, number_of_heads = (query.shape[0], query.shape[1], query.shape[2])
    block = min(SPAN, length)
    block_count = length // block

    def split_blocks(item):
        return jnp.moveaxis(
            item.reshape(seq_count, block_count, block, number_of_heads, item.shape[-1]), 1, 0
        )

    causal = (
        lax.broadcasted_iota(jnp.int32, (block, block), 0)
        >= lax.broadcasted_iota(jnp.int32, (block, block), 1)
    )[None, :, :, None, None]

    def advance(state, inputs):
        q_block, k_block, v_block, lg_block = inputs
        cumul = jnp.cumsum(lg_block, axis=1)
        spread = jnp.where(causal, cumul[:, :, None] - cumul[:, None, :], -jnp.inf)
        attention_scores = jnp.sum(
            q_block[:, :, None] * jnp.exp(spread) * k_block[:, None, :], axis=-1
        )
        inner = jnp.einsum("sijh,sjhv->sihv", attention_scores, v_block, precision=HIGH)
        outer = jnp.einsum("sihk,shkv->sihv", q_block * jnp.exp(cumul), state, precision=HIGH)
        final_log = cumul[:, -1]
        carried = jnp.exp(final_log)[..., None] * state + jnp.einsum(
            "sjhk,sjhv->shkv",
            k_block * jnp.exp(final_log[:, None] - cumul),
            v_block,
            precision=HIGH,
        )
        return (carried, inner + outer)

    start_state = jnp.zeros(
        (seq_count, number_of_heads, query.shape[-1], values.shape[-1]), jnp.float32
    )
    _, outputs = lax.scan(
        advance,
        start_state,
        tuple((split_blocks(item) for item in (query, keys, values, decay_logarithm))),
    )
    return jnp.moveaxis(outputs, 0, 1).reshape(seq_count, length, number_of_heads, values.shape[-1])


def layer(
    hidden,
    norm_gain,
    query_matrix,
    key_weight,
    value_weight,
    decay_down,
    decay_up,
    decay_bias,
    head_gain,
    output_matrix,
):
    stream = hidden.astype(jnp.float32)
    normed = normalize(stream, norm_gain[0].astype(jnp.float32)).astype(jnp.bfloat16)
    key_width = query_matrix.shape[2]
    value_width = value_weight.shape[2]
    number_of_heads = value_width // VAL
    gathered = lax.all_gather(normed, "tensor", axis=1, tiled=True)
    parts = [
        jnp.einsum("smd,df->smf", gathered, weight[0], preferred_element_type=jnp.float32).astype(
            jnp.bfloat16
        )
        for weight in (query_matrix, key_weight, value_weight, decay_down)
    ]
    joined = jnp.concatenate(parts, axis=2)
    seq_count, length = (joined.shape[0], joined.shape[1])
    query = joined[..., :key_width]
    keys = joined[..., key_width : 2 * key_width]
    values = joined[..., 2 * key_width : 2 * key_width + value_width]
    low_rank = joined[..., 2 * key_width + value_width :]
    rate_logit = (
        jnp.einsum("slr,rf->slf", low_rank, decay_up[0], preferred_element_type=jnp.float32)
        + decay_bias[0]
    )
    decay_logarithm = jax.nn.log_sigmoid(rate_logit) / 16.0
    key_shape = (seq_count, length, number_of_heads, KEY)
    mixed = blockwise(
        query.astype(jnp.float32).reshape(key_shape) * KEY ** (-0.5),
        keys.astype(jnp.float32).reshape(key_shape),
        values.astype(jnp.float32).reshape(seq_count, length, number_of_heads, VAL),
        decay_logarithm.reshape(key_shape),
    )
    head_scale = head_gain[0].astype(jnp.float32).reshape(number_of_heads, VAL)
    gated = (
        head_normalize(mixed, head_scale)
        .astype(jnp.bfloat16)
        .reshape(seq_count, length, value_width)
    )
    position_ordered = jnp.swapaxes(gated, 0, 1)
    projected = lax.psum_scatter(
        jnp.einsum(
            "kmc,cy->kmy", position_ordered, output_matrix[0], preferred_element_type=jnp.float32
        ).astype(jnp.bfloat16),
        "tensor",
        scatter_dimension=0,
        tiled=True,
    ).astype(jnp.float32)
    return (stream + jnp.swapaxes(projected, 0, 1)).astype(jnp.bfloat16)


def per_device(
    activations,
    norm_gain,
    query_matrix,
    key_weight,
    value_weight,
    decay_down,
    decay_up,
    decay_bias,
    head_gain,
    output_matrix,
):
    weights = (
        norm_gain,
        query_matrix,
        key_weight,
        value_weight,
        decay_down,
        decay_up,
        decay_bias,
        head_gain,
        output_matrix,
    )
    section_index = lax.axis_index("section")
    micro_count = activations.shape[0]
    waiting = jnp.zeros_like(activations[0])
    finished = []
    for step_index in range(micro_count + 1):
        if step_index < micro_count:
            fresh = activations[step_index]
        else:
            fresh = jnp.zeros_like(waiting)
        current = jnp.where(section_index == 0, fresh, waiting)
        produced = layer(current, *weights)
        if step_index >= 1:
            finished.append(produced)
        if step_index < micro_count:
            waiting = shifted(produced, "section", 1)
    earlier = shifted(finished[0], "section", -1)
    return jnp.where(section_index == 0, earlier, finished[-1])[None]


def solution(mesh):
    return jax.shard_map(
        per_device,
        mesh=mesh,
        in_specs=(
            P(None, "dp", "tensor", None),
            P("section", None),
            P("section", None, "tensor"),
            P("section", None, "tensor"),
            P("section", None, "tensor"),
            P("section", None, None),
            P("section", None, "tensor"),
            P("section", "tensor"),
            P("section", "tensor"),
            P("section", "tensor", None),
        ),
        out_specs=P("section", "dp", "tensor", None),
        check_vma=False,
    )
```

profile of v0, /device:TPU:2, one launch (start us, length us, event | category | flops | bytes accessed | tf_op | source)
XLA Modules:
  0.0 614.9 jit_solution(17764027246789966301)
XLA Ops:
  6.5 1.2 fusion.251
  8.5 1.6 fusion.253
  10.9 73.5 %all-gather.4.cloned.1.call-done = bf16[1,256,3584]{2,1,0:T(8,128)(2,1)} async-done(((bf16[1,16,3584]{2,1,0:T(8,128)(2,1)}), bf16[1,256,3584]{2,1,0:T(8,128)(2,1)}) %all-gather.4.cloned.1.call-update) | async-done | bytes 1835024 | tf_op jit(solution)/shard_map/all_gather | solution.py:93
  84.4 2.6 fusion.226
  88.0 3.7 fusion.107
  92.7 2.7 fusion.155
  96.4 2.1 fusion.140
  99.7 31.0 %while.39 = (s32[]{:T(128)}, f32[1,4,64,128]{3,2,1,0:T(8,128)S(1)}, f32[4,1,64,4,128]{4,2,3,1,0:T(8,128)S(1)}, f32[4,1,64,4,64]{4,3,2,1,0:T(4,128)}, f32[4,1,64,...) while((s32[]{:T(128)}, f32[1,4,64,128]{3,2,1,0:T(8,128)S(1)}, ...), condition=%wide.region_4.5_spmd.clone, body=%wide.region_1.4_spmd.clone.sunk | while | flops 81973248 | bytes 2833012 | solution.py:68
  100.7 1.1 exponential_multiply_fusion.9
  101.8 3.7 multiply_reduce_fusion.9
  108.4 1.1 exponential_multiply_fusion.9
  109.6 3.7 multiply_reduce_fusion.9
  116.2 1.1 exponential_multiply_fusion.9
  117.3 3.7 multiply_reduce_fusion.9
  125.1 3.7 multiply_reduce_fusion.9
  131.4 4.4 fusion.63
  135.9 71.0 %reduce-scatter.4.cloned.1.call-done = bf16[16,1,3584]{2,0,1:T(8,128)(2,1)} async-done(((bf16[256,1,3584]{2,0,1:T(8,128)(2,1)}), bf16[16,1,3584]{2,0,1:T(8,128)(2,1)}) %reduce-scatter.4.cloned.1.call-update) | async-done | bytes 114704 | tf_op jit(solution)/shard_map/reduce_scatter | solution.py:125
  207.8 4.5 collective-permute-start
  212.3 2.3 collective-permute-done
  215.9 68.4 %all-gather.6.cloned.1.call-done = bf16[1,256,3584]{2,1,0:T(8,128)(2,1)} async-done(((bf16[1,16,3584]{2,1,0:T(8,128)(2,1)}), bf16[1,256,3584]{2,1,0:T(8,128)(2,1)}) %all-gather.6.cloned.1.call-update) | async-done | bytes 1835024 | tf_op jit(solution)/shard_map/all_gather | solution.py:93
  284.3 3.7 fusion.117
  289.0 2.5 fusion.228
  292.5 2.1 fusion.165
  295.7 2.7 fusion.180
  299.5 31.0 %while.40 = (s32[]{:T(128)}, f32[1,4,64,128]{3,2,1,0:T(8,128)S(1)}, f32[4,1,64,4,128]{4,2,3,1,0:T(8,128)S(1)}, f32[4,1,64,4,64]{4,3,2,1,0:T(4,128)}, f32[4,1,64,...) while((s32[]{:T(128)}, f32[1,4,64,128]{3,2,1,0:T(8,128)S(1)}, ...), condition=%wide.region_11.12_spmd.clone, body=%wide.region_8.11_spmd.clone.sunk | while | flops 81973248 | bytes 2833012 | solution.py:68
  301.6 3.7 multiply_reduce_fusion.10
  309.4 3.7 multiply_reduce_fusion.10
  317.1 3.7 multiply_reduce_fusion.10
  324.9 3.7 multiply_reduce_fusion.10
  331.2 4.4 fusion.64
  335.7 70.9 %reduce-scatter.6.cloned.1.call-done = bf16[16,1,3584]{2,0,1:T(8,128)(2,1)} async-done(((bf16[256,1,3584]{2,0,1:T(8,128)(2,1)}), bf16[16,1,3584]{2,0,1:T(8,128)(2,1)}) %reduce-scatter.6.cloned.1.call-update) | async-done | bytes 114704 | tf_op jit(solution)/shard_map/reduce_scatter | solution.py:125
  407.5 4.7 collective-permute-start.2
  412.2 2.3 collective-permute-done.2
  415.7 68.4 %all-gather.8.cloned.1.call-done = bf16[1,256,3584]{2,1,0:T(8,128)(2,1)} async-done(((bf16[1,16,3584]{2,1,0:T(8,128)(2,1)}), bf16[1,256,3584]{2,1,0:T(8,128)(2,1)}) %all-gather.8.cloned.1.call-update) | async-done | bytes 1835024 | tf_op jit(solution)/shard_map/all_gather | solution.py:93
  484.2 3.7 fusion.127
  488.9 2.5 fusion.230
  492.4 2.1 fusion.190
  495.6 2.7 fusion.205
  499.4 31.0 %while.41 = (s32[]{:T(128)}, f32[1,4,64,128]{3,2,1,0:T(8,128)S(1)}, f32[4,1,64,4,128]{4,2,3,1,0:T(8,128)S(1)}, f32[4,1,64,4,64]{4,3,2,1,0:T(4,128)}, f32[4,1,64,...) while((s32[]{:T(128)}, f32[1,4,64,128]{3,2,1,0:T(8,128)S(1)}, ...), condition=%wide.region_18.19_spmd.clone, body=%wide.region_15.18_spmd.clone.sunk | while | flops 81973248 | bytes 2833012 | solution.py:68
  501.5 3.7 multiply_reduce_fusion.11
  509.3 3.7 multiply_reduce_fusion.11
  517.0 3.7 multiply_reduce_fusion.11
  524.8 3.7 multiply_reduce_fusion.11
  531.1 4.4 fusion.65
  535.5 1.3 collective-permute-start.1
  536.8 6.9 %collective-permute-done.1 = bf16[1,16,3584]{2,1,0:T(8,128)(2,1)S(1)} collective-permute-done((bf16[1,16,3584]{2,1,0:T(8,128)(2,1)S(1)}, bf16[1,16,3584]{2,1,0:T(8,128)(2,1)S(1)}, u32[]{:S(2)}, u32[]{:S(2)}) %collective-permute-start.1) | collective-permute-done | bytes 114720 | tf_op jit(solution)/shard_map/ppermute | solution.py:17
  543.7 62.8 %reduce-scatter.8.cloned.1.call-done = bf16[16,1,3584]{2,0,1:T(8,128)(2,1)} async-done(((bf16[256,1,3584]{2,0,1:T(8,128)(2,1)}), bf16[16,1,3584]{2,0,1:T(8,128)(2,1)}) %reduce-scatter.8.cloned.1.call-update) | async-done | bytes 114704 | tf_op jit(solution)/shard_map/reduce_scatter | solution.py:125
  606.5 1.6 fusion.256
  (192 shorter events, 64.3 us)
Async XLA Ops:
  6.5 89.9 %copy-start = (bf16[1,3584,256]{2,1,0:T(8,128)(2,1)S(1)}, bf16[1,3584,256]{2,1,0:T(8,128)(2,1)}, u32[]{:S(2)}) copy-start(bf16[1,3584,256]{2,1,0:T(8,128)(2,1)} %param.19) | copy-start | bytes 5505028
  6.5 77.9 %all-gather.4.cloned.1.call-start = ((), (), s32[]{:S(2)}) async-start(), calls=%async_computation.3 | async-start | bytes 1949696 | tf_op jit(solution)/shard_map/all_gather | solution.py:93
  10.1 196.7 %reduce-scatter.4.cloned.1.call-start = ((), (), s32[]{:S(2)}) async-start(), calls=%async_computation.4 | async-start | bytes 1949696 | tf_op jit(solution)/shard_map/reduce_scatter | solution.py:125
  135.8 71.1 %copy-start.1 = (bf16[2,1,16,3584]{3,2,1,0:T(8,128)(2,1)S(1)}, bf16[2,1,16,3584]{3,2,1,0:T(8,128)(2,1)}, u32[]{:S(2)}) copy-start(bf16[2,1,16,3584]{3,2,1,0:T(8,128)(2,1)} %param.16) | copy-start | bytes 688132
  135.8 148.5 %all-gather.6.cloned.1.call-start = ((), (), s32[]{:S(2)}) async-start(), calls=%async_computation.5 | async-start | bytes 1949696 | tf_op jit(solution)/shard_map/all_gather | solution.py:93
  207.8 6.9 %collective-permute-start = (bf16[1,16,3584]{2,1,0:T(8,128)(2,1)S(1)}, bf16[1,16,3584]{2,1,0:T(8,128)(2,1)S(1)}, u32[]{:S(2)}, u32[]{:S(2)}) collective-permute-start(bf16[1,16,3584]{2,1,0:T(8,128)(2,1)S(1)} %fusion.254), channel_id=1, source_target_pairs={{0,128},{1,129},{2,130},{3,131},{4,132},{5,133},{6,134},{7,135},{8... | collective-permute-start | bytes 344072 | tf_op jit(solution)/shard_map/ppermute | solution.py:17
  215.6 191.0 %reduce-scatter.6.cloned.1.call-start = ((), (), s32[]{:S(2)}) async-start(), calls=%async_computation.6 | async-start | bytes 1949696 | tf_op jit(solution)/shard_map/reduce_scatter | solution.py:125
  215.9 73.1 %copy-start.2 = (bf16[1,3584,16]{1,2,0:T(8,128)(2,1)S(1)}, bf16[1,3584,16]{1,2,0:T(8,128)(2,1)}, u32[]{:S(2)}) copy-start(bf16[1,3584,16]{1,2,0:T(8,128)(2,1)} %param.21) | copy-start | bytes 344068
  215.9 73.1 %copy-start.3 = (bf16[1,16,256]{2,1,0:T(8,128)(2,1)S(1)}, bf16[1,16,256]{2,1,0:T(8,128)(2,1)}, u32[]{:S(2)}) copy-start(bf16[1,16,256]{2,1,0:T(8,128)(2,1)} %param.22) | copy-start | bytes 24580
  215.9 73.1 %copy-start.4 = (f32[1,256]{1,0:T(1,128)S(1)}, f32[1,256]{1,0:T(1,128)}, u32[]{:S(2)}) copy-start(f32[1,256]{1,0:T(1,128)} %param.23) | copy-start | bytes 3076
  335.6 148.5 %all-gather.8.cloned.1.call-start = ((), (), s32[]{:S(2)}) async-start(), calls=%async_computation.7 | async-start | bytes 1949696 | tf_op jit(solution)/shard_map/all_gather | solution.py:93
  407.5 7.0 %collective-permute-start.2 = (bf16[1,16,3584]{2,1,0:T(8,128)(2,1)S(1)}, bf16[1,16,3584]{2,1,0:T(8,128)(2,1)S(1)}, u32[]{:S(2)}, u32[]{:S(2)}) collective-permute-start(bf16[1,16,3584]{2,1,0:T(8,128)(2,1)S(1)} %fusion.246), channel_id=1, source_target_pairs={{0,128},{1,129},{2,130},{3,131},{4,132},{5,133},{6,134},{7,135},{8... | collective-permute-start | bytes 344072 | tf_op jit(solution)/shard_map/ppermute | solution.py:17
  415.5 191.0 %reduce-scatter.8.cloned.1.call-start = ((), (), s32[]{:S(2)}) async-start(), calls=%async_computation.8 | async-start | bytes 1949696 | tf_op jit(solution)/shard_map/reduce_scatter | solution.py:125
  535.5 8.2 %collective-permute-start.1 = (bf16[1,16,3584]{2,1,0:T(8,128)(2,1)S(1)}, bf16[1,16,3584]{2,1,0:T(8,128)(2,1)S(1)}, u32[]{:S(2)}, u32[]{:S(2)}) collective-permute-start(bf16[1,16,3584]{2,1,0:T(8,128)(2,1)S(1)} %fusion.246), channel_id=1, source_target_pairs={{128,0},{129,1},{130,2},{131,3},{132,4},{133,5},{134,6},{135,7},{1... | collective-permute-start | bytes 344072 | tf_op jit(solution)/shard_map/ppermute | solution.py:17
Sparse Core Ops, SparseCore 0:
  10.3 74.0 all-gather.3
  135.9 70.8 reduce-scatter.3
  215.7 68.4 all-gather.5
  335.7 70.7 reduce-scatter.5
  415.6 68.5 all-gather.7
  535.6 70.8 reduce-scatter.7
where the time goes:
time: 616 us; the launch traced here: 615 us
  waiting for transfers between devices  427 us (69%)
  other arithmetic  80.4 us (13%)
  matrix products  57.4 us (9%)
  local copies, waits for them, and re-layouts  24.5 us (4%)
  between operations  13.8 us (2%)
  starting transfers between devices  11.1 us (2%)
    all_gather x3, waiting for transfers between devices, layer(): gathered = lax.all_gather(normed, 'tensor', axis=1, tiled=True)  210 us
    reduce_scatter x3, waiting for transfers between devices, layer(): lax.psum_scatter(jnp.einsum('kmc,cy->kmy', position_ordered, output_matri...  205 us
    reduce_sum x12, other arithmetic, advance(): jnp.sum(q_block[:, :, None] * jnp.exp(spread) * k_block[:, None, :], axis...  44.7 us
    dot_general x9, matrix products, layer(): jnp.einsum('smd,df->smf', gathered, weight[0], preferred_element_type=jnp...  25.6 us
    dot_general x3, matrix products, layer(): jnp.einsum('kmc,cy->kmy', position_ordered, output_matrix[0], preferred_e...  13.2 us
    mul x12, other arithmetic, advance(): q_block * jnp.exp(cumul)  13 us
  transfers between devices with their start and end apart: 9, of which 9 were waited for; matrix products, arithmetic and copies ran while one was open for 0% of the time, Pallas kernels for 0%

commit v1 on v0

v1 whole, which is shorter than its diff:
```python
import functools

import jax
import jax.numpy as jnp
from jax import lax
from jax.experimental import pallas as pl
from jax.experimental.pallas import tpu as pltpu
from jax.sharding import PartitionSpec as P

Z = 8
KEY = 64
VAL = 128
LEN = 256
RANK = 16
PACK = 40
OFFSETS = (0, 1, 2, 3, 5, 6, 7)
ALL = ("section", "dp", "tensor")


def zp(value):
    return lax.ppermute(value, "tensor", [(y * Z + z, y * Z + (z + 1) % Z) for y in range(2) for z in range(Z)])


def zm(value):
    return lax.ppermute(value, "tensor", [(y * Z + z, y * Z + (z + Z - 1) % Z) for y in range(2) for z in range(Z)])


def yswap(value):
    return lax.ppermute(value, "tensor", [(t, t ^ Z) for t in range(2 * Z)])


def to_second(value):
    n = 2 * Z
    return lax.ppermute(value, ("section", "tensor"), [(t, n + (t ^ Z)) for t in range(n)])


def to_first(value, cores):
    n, dp = 2 * Z, lax.axis_size("dp")
    pairs = [(dp * n + d * n + t, d * n + (t ^ Z)) for d in range(dp) if d % 2 in cores for t in range(n)]
    return lax.ppermute(value, ALL, pairs)


def to_sibling(value, core):
    dp = lax.axis_size("dp")
    return lax.ppermute(value, ("section", "dp"), [(d, d ^ 1) for d in range(dp) if d % 2 == core])


def normalize(values, gain):
    return values * lax.rsqrt(jnp.mean(values * values, axis=-1, keepdims=True) + 1e-05) * gain


def gather_ring(block):
    half = block.shape[0] // 2
    p1, m1 = zp(block), zm(block)
    p2, m2 = zp(p1), zm(m1)
    p3, m3 = zp(p2), zm(m2)
    p4, m4 = zp(p3[:half]), zm(m3[half:])
    return {0: block, 7: p1, 6: p2, 5: p3, 1: m1, 2: m2, 3: m3}, p4, m4


def add(a, b):
    return (a.astype(jnp.float32) + b.astype(jnp.float32)).astype(jnp.bfloat16)


def scatter_ring(terms, four_a, four_b):
    half = four_a.shape[0]
    p, m = zp(four_a), zm(four_b)
    up = jnp.concatenate([add(terms[3][:half], p), terms[3][half:]], 0)
    down = jnp.concatenate([terms[5][:half], add(terms[5][half:], m)], 0)
    p, m = zp(up), zm(down)
    p, m = zp(add(terms[2], p)), zm(add(terms[6], m))
    p, m = zp(add(terms[1], p)), zm(add(terms[7], m))
    return terms[0].astype(jnp.float32) + p.astype(jnp.float32) + m.astype(jnp.float32)


def nt(a, b):
    return lax.dot_general(a, b, (((1,), (1,)), ((), ())), preferred_element_type=jnp.float32)


def mix(q, k, v, low, up, bias, gain):
    width = q.shape[1]
    heads = width // KEY
    half = LEN // 2
    logits = jnp.dot(low, up, preferred_element_type=jnp.float32) + bias
    log_sig = jnp.minimum(logits, 0.0) - jnp.log1p(jnp.exp(-jnp.abs(logits)))
    decay = jnp.exp(log_sig * (1.0 / 16.0))
    q = q.astype(jnp.float32) * KEY ** -0.5
    k = k.astype(jnp.float32)
    row = lax.broadcasted_iota(jnp.int32, (LEN, width), 0)
    lane_head = lax.broadcasted_iota(jnp.int32, (1, width), 1) // KEY
    head_masks = [jnp.where(lane_head == h, 1.0, 0.0).astype(jnp.bfloat16) for h in range(heads)]
    i = lax.broadcasted_iota(jnp.int32, (heads, half, half), 1)
    j = lax.broadcasted_iota(jnp.int32, (heads, half, half), 2)

    def scores(qb, kb, rows, columns):
        lhs = jnp.concatenate([qb[rows] * m for m in head_masks], axis=0)
        return nt(lhs, kb[columns]).reshape(heads, half, half)

    first, second = slice(0, half), slice(half, LEN)
    qb, kb = q.astype(jnp.bfloat16), k.astype(jnp.bfloat16)
    att = [jnp.where(i == j, scores(qb, kb, s, s), 0.0) for s in (first, second)]
    prefix, suffix, total = decay, jnp.ones_like(decay), decay
    b = 1
    while b < half:
        qb, kb = (q * prefix).astype(jnp.bfloat16), (k * suffix).astype(jnp.bfloat16)
        mask = ((i // (2 * b)) == (j // (2 * b))) & ((i & b) != 0) & ((j & b) == 0)
        att = [jnp.where(mask, scores(qb, kb, s, s), a) for s, a in zip((first, second), att)]
        upper = (row & b) != 0
        other = jnp.where(upper, pltpu.roll(total, b, 0), pltpu.roll(total, LEN - b, 0))
        prefix = jnp.where(upper, prefix * other, prefix)
        suffix = jnp.where(upper, suffix, suffix * other)
        total = total * other
        b *= 2
    qb, kb = (q * prefix).astype(jnp.bfloat16), (k * suffix).astype(jnp.bfloat16)
    across = scores(qb, kb, second, first)
    outs = []
    for h in range(heads):
        vh = v[:, h * VAL:(h + 1) * VAL]
        top = jnp.dot(att[0][h].astype(jnp.bfloat16), vh[first], preferred_element_type=jnp.float32)
        low_part = jnp.concatenate([across[h], att[1][h]], axis=1).astype(jnp.bfloat16)
        bottom = jnp.dot(low_part, vh, preferred_element_type=jnp.float32)
        mixed = jnp.concatenate([top, bottom], axis=0)
        scale = lax.rsqrt(jnp.maximum(jnp.mean(mixed * mixed, axis=-1, keepdims=True), 1.0))
        outs.append((mixed * scale * gain[:, h * VAL:(h + 1) * VAL]).astype(jnp.bfloat16))
    return jnp.concatenate(outs, axis=1)


def layer_kernel(groups, n_sources, scalars, *refs):
    at = 0

    def take(count):
        nonlocal at
        out = refs[at:at + count]
        at += count
        return out

    blocks = take(9)
    pack, = take(1)
    sources = [take(n_sources) for _ in range(4)]
    outs = take(9)
    x, w, wo, terms, y, gated, in_sem, w_sem, out_sem = take(9)
    half = groups // 2
    z = scalars[0]
    depth = x.shape[2]

    def rows(offset):
        return pl.ds(pl.multiple_of(lax.rem(z + offset, Z) * 16, 16), 16)

    q_src, k_src, v_src, o_src = sources
    wide = w.shape[2]
    targets = [
        (q_src, slice(None), w.at[0]),
        (k_src, slice(None), w.at[1]),
        (v_src, pl.ds(0, wide), w.at[2]),
        (v_src, pl.ds(wide, wide), w.at[3]),
        (o_src, slice(None), wo),
    ]
    picks = [0, 1, 0, 0, 1]

    def weight_copy(index, which):
        src, columns, dst = targets[index]
        return pltpu.make_async_copy(src[which].at[:, columns], dst, w_sem.at[index])

    def start_weight(index):
        if n_sources == 1:
            weight_copy(index, 0).start()
            return
        choice = scalars[1 + picks[index]]
        for which in range(n_sources):
            @pl.when(choice == which)
            def _():
                weight_copy(index, which).start()

    ins = []
    for n, offset in enumerate(OFFSETS):
        ins.append(pltpu.make_async_copy(blocks[n], x.at[:, rows(offset), :], in_sem.at[n]))
    ins.append(pltpu.make_async_copy(blocks[7], x.at[pl.ds(0, half), rows(4), :], in_sem.at[7]))
    ins.append(pltpu.make_async_copy(blocks[8], x.at[pl.ds(half, half), rows(4), :], in_sem.at[8]))
    for c in ins:
        c.start()
    for index in range(5):
        start_weight(index)
    for c in ins:
        c.wait()

    xs = x.reshape(groups * 128, depth)
    down = pack[0:RANK, :].astype(jnp.bfloat16)
    low = nt(xs[...], down).astype(jnp.bfloat16)
    for index in range(4):
        weight_copy(index, 0).wait()
        y[index] = jnp.dot(xs[...], w[index], preferred_element_type=jnp.float32).astype(jnp.bfloat16)
    hg = pack[17:18, 0:2 * wide]
    bias = pack[18:19, 0:wide]
    up = pack[24:24 + RANK, 0:wide].astype(jnp.bfloat16)
    for n in range(groups // 2):
        s = slice(n * LEN, (n + 1) * LEN)
        v = jnp.concatenate([y[2, s, :], y[3, s, :]], axis=1)
        gated[s, :] = mix(y[0, s, :], y[1, s, :], v, low[s], up, bias, hg)
    weight_copy(4, 0).wait()
    ts = terms.reshape(groups * 128, depth)
    step = 512
    for c in range(depth // step):
        cols = slice(c * step, (c + 1) * step)
        ts[:, cols] = jnp.dot(gated[...], wo[:, cols], preferred_element_type=jnp.float32).astype(jnp.bfloat16)
    done = []
    for n, offset in enumerate(OFFSETS):
        done.append(pltpu.make_async_copy(terms.at[:, rows(offset), :], outs[n], out_sem.at[n]))
    done.append(pltpu.make_async_copy(terms.at[pl.ds(0, half), rows(4), :], outs[7], out_sem.at[7]))
    done.append(pltpu.make_async_copy(terms.at[pl.ds(half, half), rows(4), :], outs[8], out_sem.at[8]))
    for c in done:
        c.start()
    for c in done:
        c.wait()


def layer_call(scalars, gathered, pack, sources):
    by_offset, p4, m4 = gathered
    groups, _, depth = by_offset[0].shape
    n_sources = len(sources[0])
    count = groups * 128
    bf = jnp.bfloat16
    full = jax.ShapeDtypeStruct((groups, 16, depth), bf)
    part = jax.ShapeDtypeStruct((groups // 2, 16, depth), bf)
    anywhere = pl.BlockSpec(memory_space=pl.ANY)
    wide = sources[0][0].shape[1]
    operands = [by_offset[o] for o in OFFSETS] + [p4, m4, pack] + [a for s in sources for a in s]
    specs = [anywhere] * 9 + [pl.BlockSpec(memory_space=pltpu.VMEM)] + [anywhere] * (4 * n_sources)
    outs = pl.pallas_call(
        functools.partial(layer_kernel, groups, n_sources),
        out_shape=[full] * 7 + [part] * 2,
        in_specs=[pl.BlockSpec(memory_space=pltpu.SMEM)] + specs,
        out_specs=[anywhere] * 9,
        scratch_shapes=[
            pltpu.VMEM((groups, 128, depth), bf),
            pltpu.VMEM((4, depth, wide), bf),
            pltpu.VMEM((2 * wide, depth), bf),
            pltpu.VMEM((groups, 128, depth), bf),
            pltpu.VMEM((4, count, wide), bf),
            pltpu.VMEM((count, 2 * wide), bf),
            pltpu.SemaphoreType.DMA((9,)),
            pltpu.SemaphoreType.DMA((5,)),
            pltpu.SemaphoreType.DMA((9,)),
        ],
        compiler_params=pltpu.CompilerParams(vmem_limit_bytes=44 * 1024 * 1024),
        cost_estimate=pl.CostEstimate(
            flops=2 * count * depth * 6 * wide, bytes_accessed=12 * depth * wide + 4 * count * depth,
            transcendentals=count * wide * 3,
        ),
    )(scalars, *operands)
    return dict(zip(OFFSETS, outs[:7])), outs[7], outs[8]


def make_pack(norm_gain, decay_down, decay_up, decay_bias, head_gain):
    depth = norm_gain.shape[0]

    def wide(rows):
        rows = rows.astype(jnp.float32)
        return jnp.pad(rows, ((0, 0), (0, depth - rows.shape[1])))

    return jnp.concatenate([
        decay_down.T.astype(jnp.float32),
        norm_gain[None].astype(jnp.float32),
        wide(head_gain[None]),
        wide(decay_bias[None]),
        jnp.zeros((24 - RANK - 3, depth), jnp.float32),
        wide(decay_up),
    ], axis=0)


def per_device(activations, norm_gain, query_matrix, key_weight, value_weight, decay_down, decay_up,
               decay_bias, head_gain, output_matrix):
    section = lax.axis_index("section")
    core = lax.axis_index("dp") % 2
    tensor = lax.axis_index("tensor")
    y, z = tensor // Z, tensor % Z
    q, k, v, o = query_matrix[0], key_weight[0], value_weight[0], output_matrix[0]
    pack = make_pack(norm_gain[0], decay_down[0], decay_up[0], decay_bias[0], head_gain[0])

    pack_x = to_first(pack, (0, 1))
    v_x, k_x = to_first(v, (0,)), to_first(k, (1,))
    o_x, q_x = to_first(o, (1,)), to_first(q, (0,))
    v_d, k_d = to_sibling(v_x, 0), to_sibling(k_x, 1)
    o_d, q_d = to_sibling(o_x, 1), to_sibling(q_x, 0)

    mine = activations[:, 0]
    other = yswap(mine)
    pair = jnp.stack([jnp.where(y == 0, mine, other), jnp.where(y == 0, other, mine)], axis=1)
    normed = normalize(pair.astype(jnp.float32), norm_gain[0].astype(jnp.float32)).astype(jnp.bfloat16)
    gathered = gather_ring(normed.reshape(4, 16, -1))
    zero = jnp.zeros((), jnp.int32)
    scalars = jnp.stack([z, zero, zero]).astype(jnp.int32)
    terms = layer_call(scalars, gathered, pack, [(q,), (k,), (v,), (o,)])
    summed = scatter_ring(*terms).astype(jnp.bfloat16).reshape(2, 2, 16, -1)

    crossed = to_second(summed[1])
    own = jnp.where(section == 0, summed[0], crossed)
    partner = yswap(own)
    stream = jnp.where(section == 0, pair[0], pair[1]).astype(jnp.float32)
    stream = (stream + (own.astype(jnp.float32) + partner.astype(jnp.float32))).astype(jnp.bfloat16)
    pack_second = jnp.where(section == 0, pack_x, pack)
    normed = normalize(stream.astype(jnp.float32), pack_second[RANK]).astype(jnp.bfloat16)
    gathered = gather_ring(normed)
    pick_qv = jnp.where(section == 1, 0, jnp.where(core == 0, 1, 2))
    pick_ko = jnp.where(section == 1, 0, jnp.where(core == 1, 1, 2))
    scalars = jnp.stack([z, pick_qv, pick_ko]).astype(jnp.int32)
    terms = layer_call(scalars, gathered, pack_second, [(q, q_x, q_d), (k, k_x, k_d), (v, v_x, v_d), (o, o_x, o_d)])
    summed = scatter_ring(*terms)
    keep = jnp.where(y == 0, summed[0], summed[1])
    give = jnp.where(y == 0, summed[1], summed[0]).astype(jnp.bfloat16)
    got = yswap(give)
    base = jnp.where(y == 0, stream[0], stream[1]).astype(jnp.float32)
    return (base + (keep + got.astype(jnp.float32))).astype(jnp.bfloat16)[None, None]


def solution(mesh):
    return jax.shard_map(
        per_device,
        mesh=mesh,
        in_specs=(
            P(None, "dp", "tensor", None),
            P("section", None),
            P("section", None, "tensor"),
            P("section", None, "tensor"),
            P("section", None, "tensor"),
            P("section", None, None),
            P("section", None, "tensor"),
            P("section", "tensor"),
            P("section", "tensor"),
            P("section", "tensor", None),
        ),
        out_specs=P("section", "dp", "tensor", None),
        check_vma=False,
    )
```

time: 616 us -> 335 us (0.54)
  waiting for transfers between devices: 427 us -> 193 us
  other arithmetic: 80.4 us -> 7.04 us
  starting transfers between devices: 11.1 us -> 79.3 us
  matrix products: 57.4 us -> 0 us
  Pallas kernels: 0 us -> 30.1 us
  between operations: 13.8 us -> 0.69 us
    all_gather x3 -> x0, waiting for transfers between devices: 210 us -> none  [layer(): gathered = lax.all_gather(normed, 'tensor', axis=1, tiled=True)]
    reduce_scatter x3 -> x0, waiting for transfers between devices: 205 us -> none  [layer(): lax.psum_scatter(jnp.einsum('kmc,cy->kmy', position_ordered, output_matri...]
    ppermute x3 -> x45, waiting for transfers between devices: 11.6 us -> 193 us  [the longest x16 78.1 us: zp(): lax.ppermute(value, 'tensor', [(y * Z + z, y * Z + (z + 1) % Z) for y in...]
    ppermute x3 -> x45, starting transfers between devices: 10.5 us -> 79.3 us  [the longest x16 48.6 us: zm(): lax.ppermute(value, 'tensor', [(y * Z + z, y * Z + (z + Z - 1) % Z) for y...]
    dot_general x51 -> x0, matrix products: 57.4 us -> none  [the longest x9 25.6 us: layer(): jnp.einsum('smd,df->smf', gathered, weight[0], preferred_element_type=jnp...]
    reduce_sum x15 -> x0, other arithmetic: 45.4 us -> none  [the longest x12 44.7 us: advance(): jnp.sum(q_block[:, :, None] * jnp.exp(spread) * k_block[:, None, :], axis...]
    pallas_call x0 -> x2, Pallas kernels: none -> 30.1 us  [layer_call(): pl.pallas_call(functools.partial(layer_kernel, groups, n_sources), out_sh...]
    mul x12 -> x0, other arithmetic: 13 us -> none  [advance(): q_block * jnp.exp(cumul)]
  transfers between devices with their start and end apart: 9 -> 45, of which waited for: 9 -> 30; matrix products, arithmetic and copies ran while one was open for 0% -> 3% of each run, Pallas kernels for 0% -> 0%
where the time goes in v1:
time: 335 us; the launch traced here: 328 us
  waiting for transfers between devices  193 us (58%)
  starting transfers between devices  79.3 us (24%)
  Pallas kernels  30.1 us (9%)
  local copies, waits for them, and re-layouts  18.4 us (5%)
  other arithmetic  7.04 us (2%)
    ppermute x16, waiting for transfers between devices, zp(): lax.ppermute(value, 'tensor', [(y * Z + z, y * Z + (z + 1) % Z) for y in...  78.1 us
    ppermute x5, waiting for transfers between devices, to_first(): return lax.ppermute(value, ALL, pairs)  62 us
    ppermute x16, starting transfers between devices, zm(): lax.ppermute(value, 'tensor', [(y * Z + z, y * Z + (z + Z - 1) % Z) for y...  48.6 us
    ppermute x16, waiting for transfers between devices, zm(): lax.ppermute(value, 'tensor', [(y * Z + z, y * Z + (z + Z - 1) % Z) for y...  43.2 us
    pallas_call x2, Pallas kernels, layer_call(): pl.pallas_call(functools.partial(layer_kernel, groups, n_sources), out_sh...  30.1 us
    unnamed x52, local copies, waits for them, and re-layouts  12.8 us
    ppermute x1, starting transfers between devices, to_second(): lax.ppermute(value, ('section', 'tensor'), [(t, n + (t ^ Z)) for t in ran...  10.1 us
    ppermute x3, waiting for transfers between devices, yswap(): return lax.ppermute(value, 'tensor', [(t, t ^ Z) for t in range(2 * Z)])  9.65 us
  transfers between devices with their start and end apart: 45, of which 30 were waited for; matrix products, arithmetic and copies ran while one was open for 3% of the time, Pallas kernels for 0%

profile of v1, /device:TPU:2, one launch (start us, length us, event | category | flops | bytes accessed | tf_op | source)
XLA Modules:
  0.0 328.4 jit_solution(5365577725954621626)
XLA Ops:
  0.0 1.7 collective-permute-start
  2.5 5.2 %collective-permute-done = bf16[2,16,3584]{2,1,0:T(8,128)(2,1)S(1)} collective-permute-done((bf16[2,16,3584]{2,1,0:T(8,128)(2,1)}, bf16[2,16,3584]{2,1,0:T(8,128)(2,1)S(1)}, u32[]{:S(2)}, u32[]{:S(2)}) %collective-permute-start) | collective-permute-done | bytes 229408 | tf_op jit(solution)/shard_map/ppermute | solution.py:29
  9.6 2.0 collective-permute-start.4
  11.6 4.0 %collective-permute-start.1 = (bf16[4,16,3584]{2,1,0:T(8,128)(2,1)S(1)}, bf16[4,16,3584]{2,1,0:T(8,128)(2,1)S(1)}, u32[]{:S(2)}, u32[]{:S(2)}) collective-permute-start(bf16[4,16,3584]{2,1,0:T(8,128)(2,1)S(1)} %fusion.1.refs_0_), channel_id=1, source_target_pairs={{0,7},{1,0},{2,1},{3,2},{4,3},{5,4},{6,5},{7,6},{8,15},{9,8},{10,9... | collective-permute-start | bytes 1376264 | tf_op jit(solution)/shard_map/ppermute | solution.py:25
  15.6 9.6 %collective-permute-done.4.refs_6_ = bf16[4,16,3584]{2,1,0:T(8,128)(2,1)S(1)} collective-permute-done((bf16[4,16,3584]{2,1,0:T(8,128)(2,1)S(1)}, bf16[4,16,3584]{2,1,0:T(8,128)(2,1)S(1)}, u32[]{:S(2)}, u32[]{:S(2)}) %collective-permute-start.4) | collective-permute-done | bytes 458784 | tf_op jit(solution)/shard_map/ppermute | solution.py:21
  26.0 3.2 collective-permute-start.2
  30.0 7.2 %collective-permute-done.5.refs_5_ = bf16[4,16,3584]{2,1,0:T(8,128)(2,1)} collective-permute-done((bf16[4,16,3584]{2,1,0:T(8,128)(2,1)S(1)}, bf16[4,16,3584]{2,1,0:T(8,128)(2,1)}, u32[]{:S(2)}, u32[]{:S(2)}) %collective-permute-start.5) | collective-permute-done | bytes 458784 | tf_op jit(solution)/shard_map/ppermute | solution.py:21
  37.2 3.8 %collective-permute-start.3 = (bf16[4,16,3584]{2,1,0:T(8,128)(2,1)}, bf16[4,16,3584]{2,1,0:T(8,128)(2,1)S(1)}, u32[]{:S(2)}, u32[]{:S(2)}) collective-permute-start(bf16[4,16,3584]{2,1,0:T(8,128)(2,1)} %collective-permute-done.2.refs_2_), channel_id=1, source_target_pairs={{0,7},{1,0},{2,1},{3,2},{4,3},{5,4},{6,5},{7,6},{8,15},{9,8},{10,9... | collective-permute-start | bytes 1376264 | tf_op jit(solution)/shard_map/ppermute | solution.py:25
  42.4 6.1 %collective-permute-done.6.refs_4_ = bf16[4,16,3584]{2,1,0:T(8,128)(2,1)S(1)} collective-permute-done((bf16[4,16,3584]{2,1,0:T(8,128)(2,1)}, bf16[4,16,3584]{2,1,0:T(8,128)(2,1)S(1)}, u32[]{:S(2)}, u32[]{:S(2)}) %collective-permute-start.6) | collective-permute-done | bytes 458784 | tf_op jit(solution)/shard_map/ppermute | solution.py:21
  49.9 3.4 %collective-permute-start.8 = (bf16[2,16,3584]{2,1,0:T(8,128)(2,1)}, bf16[2,16,3584]{2,1,0:T(8,128)(2,1)}, u32[]{:S(2)}, u32[]{:S(2)}) collective-permute-start(bf16[2,16,3584]{2,1,0:T(8,128)(2,1)} %slice.93), channel_id=1, source_target_pairs={{0,7},{1,0},{2,1},{3,2},{4,3},{5,4},{6,5},{7,6},{8,15},{9,8},{10,9... | collective-permute-start | bytes 688136 | tf_op jit(solution)/shard_map/ppermute | solution.py:25
  53.4 2.0 concatenate.15.refs_9_
  60.3 18.2 %shard_map.100 = (bf16[4,16,3584]{2,1,0:T(8,128)(2,1)S(1)}, bf16[4,16,3584]{2,1,0:T(8,128)(2,1)S(1)}, bf16[4,16,3584]{2,1,0:T(8,128)(2,1)S(1)}, bf16[4,16,3584]{...) custom-call(s32[3]{0:T(128)S(1)} %stack.29.scalars, ...), custom_call_target="tpu_custom_call" | custom-call | flops 5637144576 | bytes 18350080 | tf_op jit(solution)/shard_map/pallas_call | solution.py:228
  78.4 3.8 %collective-permute-start.13 = (bf16[2,16,3584]{2,1,0:T(8,128)(2,1)S(1)}, bf16[2,16,3584]{2,1,0:T(8,128)(2,1)S(1)}, u32[]{:S(2)}, u32[]{:S(2)}) collective-permute-start(bf16[2,16,3584]{2,1,0:T(8,128)(2,1)S(1)} %get-tuple-element.31), channel_id=1, source_target_pairs={{0,7},{1,0},{2,1},{3,2},{4,3},{5,4},{6,5},{7,6},{8,15},{9,8},{10,9... | collective-permute-start | bytes 688136 | tf_op jit(solution)/shard_map/ppermute | solution.py:25
  83.5 2.5 collective-permute-start.34
  87.0 4.2 %collective-permute-start.14 = (bf16[4,16,3584]{2,1,0:T(8,128)(2,1)S(1)}, bf16[4,16,3584]{2,1,0:T(8,128)(2,1)S(1)}, u32[]{:S(2)}, u32[]{:S(2)}) collective-permute-start(bf16[4,16,3584]{2,1,0:T(8,128)(2,1)S(1)} %pad_maximum_fusion.2), channel_id=1, source_target_pairs={{0,7},{1,0},{2,1},{3,2},{4,3},{5,4},{6,5},{7,6},{8,15},{9,8},{10,9... | collective-permute-start | bytes 1376264 | tf_op jit(solution)/shard_map/ppermute | solution.py:25
  91.2 4.5 %collective-permute-done.9 = bf16[2,16,3584]{2,1,0:T(8,128)(2,1)S(1)} collective-permute-done((bf16[2,16,3584]{2,1,0:T(8,128)(2,1)S(1)}, bf16[2,16,3584]{2,1,0:T(8,128)(2,1)S(1)}, u32[]{:S(2)}, u32[]{:S(2)}) %collective-permute-start.9) | collective-permute-done | bytes 229408 | tf_op jit(solution)/shard_map/ppermute | solution.py:21
  95.9 3.6 %collective-permute-done.14 = bf16[4,16,3584]{2,1,0:T(8,128)(2,1)S(1)} collective-permute-done((bf16[4,16,3584]{2,1,0:T(8,128)(2,1)S(1)}, bf16[4,16,3584]{2,1,0:T(8,128)(2,1)S(1)}, u32[]{:S(2)}, u32[]{:S(2)}) %collective-permute-start.14) | collective-permute-done | bytes 458784 | tf_op jit(solution)/shard_map/ppermute | solution.py:25
  99.6 3.8 %collective-permute-start.15 = (bf16[4,16,3584]{2,1,0:T(8,128)(2,1)S(1)}, bf16[4,16,3584]{2,1,0:T(8,128)(2,1)S(1)}, u32[]{:S(2)}, u32[]{:S(2)}) collective-permute-start(bf16[4,16,3584]{2,1,0:T(8,128)(2,1)S(1)} %add_convert_fusion.2), channel_id=1, source_target_pairs={{0,7},{1,0},{2,1},{3,2},{4,3},{5,4},{6,5},{7,6},{8,15},{9,8},{10,9... | collective-permute-start | bytes 1376264 | tf_op jit(solution)/shard_map/ppermute | solution.py:25
  103.4 5.3 %collective-permute-done.10 = bf16[4,16,3584]{2,1,0:T(8,128)(2,1)S(1)} collective-permute-done((bf16[4,16,3584]{2,1,0:T(8,128)(2,1)S(1)}, bf16[4,16,3584]{2,1,0:T(8,128)(2,1)S(1)}, u32[]{:S(2)}, u32[]{:S(2)}) %collective-permute-start.10) | collective-permute-done | bytes 458784 | tf_op jit(solution)/shard_map/ppermute | solution.py:21
  108.9 3.5 %collective-permute-done.15 = bf16[4,16,3584]{2,1,0:T(8,128)(2,1)S(1)} collective-permute-done((bf16[4,16,3584]{2,1,0:T(8,128)(2,1)S(1)}, bf16[4,16,3584]{2,1,0:T(8,128)(2,1)S(1)}, u32[]{:S(2)}, u32[]{:S(2)}) %collective-permute-start.15) | collective-permute-done | bytes 458784 | tf_op jit(solution)/shard_map/ppermute | solution.py:25
  112.5 3.8 %collective-permute-start.16 = (bf16[4,16,3584]{2,1,0:T(8,128)(2,1)S(1)}, bf16[4,16,3584]{2,1,0:T(8,128)(2,1)S(1)}, u32[]{:S(2)}, u32[]{:S(2)}) collective-permute-start(bf16[4,16,3584]{2,1,0:T(8,128)(2,1)S(1)} %add_convert_fusion.1), channel_id=1, source_target_pairs={{0,7},{1,0},{2,1},{3,2},{4,3},{5,4},{6,5},{7,6},{8,15},{9,8},{10,9... | collective-permute-start | bytes 1376264 | tf_op jit(solution)/shard_map/ppermute | solution.py:25
  116.2 6.2 %collective-permute-done.11 = bf16[4,16,3584]{2,1,0:T(8,128)(2,1)S(1)} collective-permute-done((bf16[4,16,3584]{2,1,0:T(8,128)(2,1)S(1)}, bf16[4,16,3584]{2,1,0:T(8,128)(2,1)S(1)}, u32[]{:S(2)}, u32[]{:S(2)}) %collective-permute-start.11) | collective-permute-done | bytes 458784 | tf_op jit(solution)/shard_map/ppermute | solution.py:21
  122.6 9.7 %collective-permute-done.12 = bf16[4,16,3584]{2,1,0:T(8,128)(2,1)S(1)} collective-permute-done((bf16[4,16,3584]{2,1,0:T(8,128)(2,1)S(1)}, bf16[4,16,3584]{2,1,0:T(8,128)(2,1)S(1)}, u32[]{:S(2)}, u32[]{:S(2)}) %collective-permute-start.12) | collective-permute-done | bytes 458784 | tf_op jit(solution)/shard_map/ppermute | solution.py:21
  133.1 10.1 %collective-permute-start.17 = (bf16[2,16,3584]{2,1,0:T(8,128)(2,1)}, bf16[2,16,3584]{2,1,0:T(8,128)(2,1)}, u32[]{:S(2)}, u32[]{:S(2)}) collective-permute-start(bf16[2,16,3584]{2,1,0:T(8,128)(2,1)} %slice.95), channel_id=1, source_target_pairs={{0,136},{1,137},{2,138},{3,139},{4,140},{5,141},{6,142},{7,143},{8... | collective-permute-start | bytes 688136 | tf_op jit(solution)/shard_map/ppermute | solution.py:34
  145.8 22.1 %collective-permute-done.32.refs_17_ = bf16[3584,512]{1,0:T(8,128)(2,1)} collective-permute-done((bf16[3584,512]{1,0:T(8,128)(2,1)}, bf16[3584,512]{1,0:T(8,128)(2,1)}, u32[]{:S(2)}, u32[]{:S(2)}) %collective-permute-start.32) | collective-permute-done | bytes 3670048 | tf_op jit(solution)/shard_map/ppermute | solution.py:40
  167.9 1.9 collective-permute-start.30
  169.8 3.2 collective-permute-start.33
  174.3 5.9 %collective-permute-done.19 = f32[40,3584]{1,0:T(8,128)} collective-permute-done((f32[40,3584]{1,0:T(8,128)S(1)}, f32[40,3584]{1,0:T(8,128)}, u32[]{:S(2)}, u32[]{:S(2)}) %collective-permute-start.19) | collective-permute-done | bytes 573472 | tf_op jit(solution)/shard_map/ppermute | solution.py:40
  181.7 34.0 %collective-permute-done.28.refs_11_ = bf16[3584,256]{1,0:T(8,128)(2,1)} collective-permute-done((bf16[3584,256]{1,0:T(8,128)(2,1)S(1)}, bf16[3584,256]{1,0:T(8,128)(2,1)}, u32[]{:S(2)}, u32[]{:S(2)}) %collective-permute-start.28) | collective-permute-done | bytes 1835040 | tf_op jit(solution)/shard_map/ppermute | solution.py:40
  218.9 8.3 %collective-permute-done.23.refs_6_ = bf16[2,16,3584]{2,1,0:T(8,128)(2,1)S(1)} collective-permute-done((bf16[2,16,3584]{2,1,0:T(8,128)(2,1)S(1)}, bf16[2,16,3584]{2,1,0:T(8,128)(2,1)S(1)}, u32[]{:S(2)}, u32[]{:S(2)}) %collective-permute-start.23) | collective-permute-done | bytes 229408 | tf_op jit(solution)/shard_map/ppermute | solution.py:21
  227.1 8.2 %collective-permute-done.20.refs_1_ = bf16[2,16,3584]{2,1,0:T(8,128)(2,1)S(1)} collective-permute-done((bf16[2,16,3584]{2,1,0:T(8,128)(2,1)S(1)}, bf16[2,16,3584]{2,1,0:T(8,128)(2,1)S(1)}, u32[]{:S(2)}, u32[]{:S(2)}) %collective-permute-start.20) | collective-permute-done | bytes 229408 | tf_op jit(solution)/shard_map/ppermute | solution.py:25
  235.3 8.8 %collective-permute-done.24.refs_5_ = bf16[2,16,3584]{2,1,0:T(8,128)(2,1)S(1)} collective-permute-done((bf16[2,16,3584]{2,1,0:T(8,128)(2,1)S(1)}, bf16[2,16,3584]{2,1,0:T(8,128)(2,1)S(1)}, u32[]{:S(2)}, u32[]{:S(2)}) %collective-permute-start.24) | collective-permute-done | bytes 229408 | tf_op jit(solution)/shard_map/ppermute | solution.py:21
  244.9 6.1 %collective-permute-done.21.refs_2_ = bf16[2,16,3584]{2,1,0:T(8,128)(2,1)S(1)} collective-permute-done((bf16[2,16,3584]{2,1,0:T(8,128)(2,1)S(1)}, bf16[2,16,3584]{2,1,0:T(8,128)(2,1)S(1)}, u32[]{:S(2)}, u32[]{:S(2)}) %collective-permute-start.21) | collective-permute-done | bytes 229408 | tf_op jit(solution)/shard_map/ppermute | solution.py:25
  251.7 6.5 %collective-permute-done.25.refs_4_ = bf16[2,16,3584]{2,1,0:T(8,128)(2,1)S(1)} collective-permute-done((bf16[2,16,3584]{2,1,0:T(8,128)(2,1)S(1)}, bf16[2,16,3584]{2,1,0:T(8,128)(2,1)S(1)}, u32[]{:S(2)}, u32[]{:S(2)}) %collective-permute-start.25) | collective-permute-done | bytes 229408 | tf_op jit(solution)/shard_map/ppermute | solution.py:21
  260.0 4.3 %collective-permute-done.22.refs_3_ = bf16[2,16,3584]{2,1,0:T(8,128)(2,1)S(1)} collective-permute-done((bf16[2,16,3584]{2,1,0:T(8,128)(2,1)S(1)}, bf16[2,16,3584]{2,1,0:T(8,128)(2,1)S(1)}, u32[]{:S(2)}, u32[]{:S(2)}) %collective-permute-start.22) | collective-permute-done | bytes 229408 | tf_op jit(solution)/shard_map/ppermute | solution.py:25
  266.1 3.4 %collective-permute-start.27 = (bf16[1,16,3584]{2,1,0:T(8,128)(2,1)}, bf16[1,16,3584]{2,1,0:T(8,128)(2,1)S(1)}, u32[]{:S(2)}, u32[]{:S(2)}) collective-permute-start(bf16[1,16,3584]{2,1,0:T(8,128)(2,1)} %slice.100), channel_id=1, source_target_pairs={{0,7},{1,0},{2,1},{3,2},{4,3},{5,4},{6,5},{7,6},{8,15},{9,8},{10,9... | collective-permute-start | bytes 344072 | tf_op jit(solution)/shard_map/ppermute | solution.py:25
  270.4 1.8 collective-permute-done.27.refs_8_
  276.5 11.9 %shard_map.101 = (bf16[2,16,3584]{2,1,0:T(8,128)(2,1)S(1)}, bf16[2,16,3584]{2,1,0:T(8,128)(2,1)S(1)}, bf16[2,16,3584]{2,1,0:T(8,128)(2,1)S(1)}, bf16[2,16,3584]{...) custom-call(s32[3]{0:T(128)S(1)} %pad_add_fusion.scalars, ...), custom_call_target="tpu_custom_call" | custom-call | flops 2818572288 | bytes 14680064 | tf_op jit(solution)/shard_map/pallas_call | solution.py:228
  288.5 3.6 %collective-permute-start.40 = (bf16[1,16,3584]{2,1,0:T(8,128)(2,1)S(1)}, bf16[1,16,3584]{2,1,0:T(8,128)(2,1)S(1)}, u32[]{:S(2)}, u32[]{:S(2)}) collective-permute-start(bf16[1,16,3584]{2,1,0:T(8,128)(2,1)S(1)} %get-tuple-element.40), channel_id=1, source_target_pairs={{0,7},{1,0},{2,1},{3,2},{4,3},{5,4},{6,5},{7,6},{8,15},{9,8},{10,9... | collective-permute-start | bytes 344072 | tf_op jit(solution)/shard_map/ppermute | solution.py:25
  292.2 3.0 collective-permute-done.40
  295.3 3.8 %collective-permute-start.41 = (bf16[2,16,3584]{2,1,0:T(8,128)(2,1)S(1)}, bf16[2,16,3584]{2,1,0:T(8,128)(2,1)S(1)}, u32[]{:S(2)}, u32[]{:S(2)}) collective-permute-start(bf16[2,16,3584]{2,1,0:T(8,128)(2,1)S(1)} %pad_maximum_fusion.4), channel_id=1, source_target_pairs={{0,7},{1,0},{2,1},{3,2},{4,3},{5,4},{6,5},{7,6},{8,15},{9,8},{10,9... | collective-permute-start | bytes 688136 | tf_op jit(solution)/shard_map/ppermute | solution.py:25
  299.2 4.5 %collective-permute-done.41 = bf16[2,16,3584]{2,1,0:T(8,128)(2,1)S(1)} collective-permute-done((bf16[2,16,3584]{2,1,0:T(8,128)(2,1)S(1)}, bf16[2,16,3584]{2,1,0:T(8,128)(2,1)S(1)}, u32[]{:S(2)}, u32[]{:S(2)}) %collective-permute-start.41) | collective-permute-done | bytes 229408 | tf_op jit(solution)/shard_map/ppermute | solution.py:25
  303.8 3.8 %collective-permute-start.42 = (bf16[2,16,3584]{2,1,0:T(8,128)(2,1)S(1)}, bf16[2,16,3584]{2,1,0:T(8,128)(2,1)S(1)}, u32[]{:S(2)}, u32[]{:S(2)}) collective-permute-start(bf16[2,16,3584]{2,1,0:T(8,128)(2,1)S(1)} %add_convert_fusion.6), channel_id=1, source_target_pairs={{0,7},{1,0},{2,1},{3,2},{4,3},{5,4},{6,5},{7,6},{8,15},{9,8},{10,9... | collective-permute-start | bytes 688136 | tf_op jit(solution)/shard_map/ppermute | solution.py:25
  307.7 3.6 %collective-permute-done.42 = bf16[2,16,3584]{2,1,0:T(8,128)(2,1)S(1)} collective-permute-done((bf16[2,16,3584]{2,1,0:T(8,128)(2,1)S(1)}, bf16[2,16,3584]{2,1,0:T(8,128)(2,1)S(1)}, u32[]{:S(2)}, u32[]{:S(2)}) %collective-permute-start.42) | collective-permute-done | bytes 229408 | tf_op jit(solution)/shard_map/ppermute | solution.py:25
  311.4 3.8 %collective-permute-start.43 = (bf16[2,16,3584]{2,1,0:T(8,128)(2,1)S(1)}, bf16[2,16,3584]{2,1,0:T(8,128)(2,1)S(1)}, u32[]{:S(2)}, u32[]{:S(2)}) collective-permute-start(bf16[2,16,3584]{2,1,0:T(8,128)(2,1)S(1)} %add_convert_fusion.5), channel_id=1, source_target_pairs={{0,7},{1,0},{2,1},{3,2},{4,3},{5,4},{6,5},{7,6},{8,15},{9,8},{10,9... | collective-permute-start | bytes 688136 | tf_op jit(solution)/shard_map/ppermute | solution.py:25
  315.3 3.4 %collective-permute-done.43 = bf16[2,16,3584]{2,1,0:T(8,128)(2,1)S(1)} collective-permute-done((bf16[2,16,3584]{2,1,0:T(8,128)(2,1)S(1)}, bf16[2,16,3584]{2,1,0:T(8,128)(2,1)S(1)}, u32[]{:S(2)}, u32[]{:S(2)}) %collective-permute-start.43) | collective-permute-done | bytes 229408 | tf_op jit(solution)/shard_map/ppermute | solution.py:25
  318.7 3.8 %collective-permute-done.39 = bf16[2,16,3584]{2,1,0:T(8,128)(2,1)S(1)} collective-permute-done((bf16[2,16,3584]{2,1,0:T(8,128)(2,1)S(1)}, bf16[2,16,3584]{2,1,0:T(8,128)(2,1)S(1)}, u32[]{:S(2)}, u32[]{:S(2)}) %collective-permute-start.39) | collective-permute-done | bytes 229408 | tf_op jit(solution)/shard_map/ppermute | solution.py:21
  323.1 4.4 %collective-permute-done.44 = bf16[16,3584]{1,0:T(8,128)(2,1)S(1)} collective-permute-done((bf16[16,3584]{1,0:T(8,128)(2,1)S(1)}, bf16[16,3584]{1,0:T(8,128)(2,1)S(1)}, u32[]{:S(2)}, u32[]{:S(2)}) %collective-permute-start.44) | collective-permute-done | bytes 114720 | tf_op jit(solution)/shard_map/ppermute | solution.py:29
  (145 shorter events, 36.8 us)
Async XLA Ops:
  0.0 57.2 %copy-start = (bf16[1,3584,256]{2,1,0:T(8,128)(2,1)S(1)}, bf16[1,3584,256]{2,1,0:T(8,128)(2,1)}, u32[]{:S(2)}) copy-start(bf16[1,3584,256]{2,1,0:T(8,128)(2,1)} %param.12) | copy-start | bytes 5505028
  0.0 7.6 %collective-permute-start = (bf16[2,16,3584]{2,1,0:T(8,128)(2,1)}, bf16[2,16,3584]{2,1,0:T(8,128)(2,1)S(1)}, u32[]{:S(2)}, u32[]{:S(2)}) collective-permute-start(bf16[2,16,3584]{2,1,0:T(8,128)(2,1)} %bitcast.56), channel_id=1, source_target_pairs={{0,8},{1,9},{2,10},{3,11},{4,12},{5,13},{6,14},{7,15},{8,0},{9,1},... | collective-permute-start | bytes 688136 | tf_op jit(solution)/shard_map/ppermute | solution.py:29
  9.6 15.6 %collective-permute-start.4 = (bf16[4,16,3584]{2,1,0:T(8,128)(2,1)S(1)}, bf16[4,16,3584]{2,1,0:T(8,128)(2,1)S(1)}, u32[]{:S(2)}, u32[]{:S(2)}) collective-permute-start(bf16[4,16,3584]{2,1,0:T(8,128)(2,1)S(1)} %fusion.1.refs_0_), channel_id=1, source_target_pairs={{0,1},{1,2},{2,3},{3,4},{4,5},{5,6},{6,7},{7,0},{8,9},{9,10},{10,1... | collective-permute-start | bytes 1376264 | tf_op jit(solution)/shard_map/ppermute | solution.py:21
  11.6 14.4 %collective-permute-start.1 = (bf16[4,16,3584]{2,1,0:T(8,128)(2,1)S(1)}, bf16[4,16,3584]{2,1,0:T(8,128)(2,1)S(1)}, u32[]{:S(2)}, u32[]{:S(2)}) collective-permute-start(bf16[4,16,3584]{2,1,0:T(8,128)(2,1)S(1)} %fusion.1.refs_0_), channel_id=1, source_target_pairs={{0,7},{1,0},{2,1},{3,2},{4,3},{5,4},{6,5},{7,6},{8,15},{9,8},{10,9... | collective-permute-start | bytes 1376264 | tf_op jit(solution)/shard_map/ppermute | solution.py:25
  25.2 12.1 %collective-permute-start.5 = (bf16[4,16,3584]{2,1,0:T(8,128)(2,1)S(1)}, bf16[4,16,3584]{2,1,0:T(8,128)(2,1)}, u32[]{:S(2)}, u32[]{:S(2)}) collective-permute-start(bf16[4,16,3584]{2,1,0:T(8,128)(2,1)S(1)} %collective-permute-done.4.refs_6_), channel_id=1, source_target_pairs={{0,1},{1,2},{2,3},{3,4},{4,5},{5,6},{6,7},{7,0},{8,9},{9,10},{10,1... | collective-permute-start | bytes 1376264 | tf_op jit(solution)/shard_map/ppermute | solution.py:21
  26.0 11.3 %collective-permute-start.2 = (bf16[4,16,3584]{2,1,0:T(8,128)(2,1)S(1)}, bf16[4,16,3584]{2,1,0:T(8,128)(2,1)}, u32[]{:S(2)}, u32[]{:S(2)}) collective-permute-start(bf16[4,16,3584]{2,1,0:T(8,128)(2,1)S(1)} %collective-permute-done.1.refs_1_), channel_id=1, source_target_pairs={{0,7},{1,0},{2,1},{3,2},{4,3},{5,4},{6,5},{7,6},{8,15},{9,8},{10,9... | collective-permute-start | bytes 1376264 | tf_op jit(solution)/shard_map/ppermute | solution.py:25
  37.2 11.2 %collective-permute-start.6 = (bf16[4,16,3584]{2,1,0:T(8,128)(2,1)}, bf16[4,16,3584]{2,1,0:T(8,128)(2,1)S(1)}, u32[]{:S(2)}, u32[]{:S(2)}) collective-permute-start(bf16[4,16,3584]{2,1,0:T(8,128)(2,1)} %collective-permute-done.5.refs_5_), channel_id=1, source_target_pairs={{0,1},{1,2},{2,3},{3,4},{4,5},{5,6},{6,7},{7,0},{8,9},{9,10},{10,1... | collective-permute-start | bytes 1376264 | tf_op jit(solution)/shard_map/ppermute | solution.py:21
  37.2 11.9 %collective-permute-start.3 = (bf16[4,16,3584]{2,1,0:T(8,128)(2,1)}, bf16[4,16,3584]{2,1,0:T(8,128)(2,1)S(1)}, u32[]{:S(2)}, u32[]{:S(2)}) collective-permute-start(bf16[4,16,3584]{2,1,0:T(8,128)(2,1)} %collective-permute-done.2.refs_2_), channel_id=1, source_target_pairs={{0,7},{1,0},{2,1},{3,2},{4,3},{5,4},{6,5},{7,6},{8,15},{9,8},{10,9... | collective-permute-start | bytes 1376264 | tf_op jit(solution)/shard_map/ppermute | solution.py:25
  49.2 7.5 %collective-permute-start.7 = (bf16[2,16,3584]{2,1,0:T(8,128)(2,1)}, bf16[2,16,3584]{2,1,0:T(8,128)(2,1)}, u32[]{:S(2)}, u32[]{:S(2)}) collective-permute-start(bf16[2,16,3584]{2,1,0:T(8,128)(2,1)} %slice.92), channel_id=1, source_target_pairs={{0,1},{1,2},{2,3},{3,4},{4,5},{5,6},{6,7},{7,0},{8,9},{9,10},{10,1... | collective-permute-start | bytes 688136 | tf_op jit(solution)/shard_map/ppermute | solution.py:21
  49.9 7.2 %collective-permute-start.8 = (bf16[2,16,3584]{2,1,0:T(8,128)(2,1)}, bf16[2,16,3584]{2,1,0:T(8,128)(2,1)}, u32[]{:S(2)}, u32[]{:S(2)}) collective-permute-start(bf16[2,16,3584]{2,1,0:T(8,128)(2,1)} %slice.93), channel_id=1, source_target_pairs={{0,7},{1,0},{2,1},{3,2},{4,3},{5,4},{6,5},{7,6},{8,15},{9,8},{10,9... | collective-permute-start | bytes 688136 | tf_op jit(solution)/shard_map/ppermute | solution.py:25
  78.4 8.5 %collective-permute-start.13 = (bf16[2,16,3584]{2,1,0:T(8,128)(2,1)S(1)}, bf16[2,16,3584]{2,1,0:T(8,128)(2,1)S(1)}, u32[]{:S(2)}, u32[]{:S(2)}) collective-permute-start(bf16[2,16,3584]{2,1,0:T(8,128)(2,1)S(1)} %get-tuple-element.31), channel_id=1, source_target_pairs={{0,7},{1,0},{2,1},{3,2},{4,3},{5,4},{6,5},{7,6},{8,15},{9,8},{10,9... | collective-permute-start | bytes 688136 | tf_op jit(solution)/shard_map/ppermute | solution.py:25
  82.2 85.7 %collective-permute-start.32 = (bf16[3584,512]{1,0:T(8,128)(2,1)}, bf16[3584,512]{1,0:T(8,128)(2,1)}, u32[]{:S(2)}, u32[]{:S(2)}) collective-permute-start(bf16[3584,512]{1,0:T(8,128)(2,1)} %bitcast.13.refs_12_.refs_16_), channel_id=1, source_target_pairs={{128,8},{129,9},{130,10},{131,11},{132,12},{133,13},{134,14},{135,... | collective-permute-start | bytes 11010056 | tf_op jit(solution)/shard_map/ppermute | solution.py:40
  83.5 86.3 %collective-permute-start.34 = (bf16[512,3584]{1,0:T(8,128)(2,1)}, bf16[512,3584]{1,0:T(8,128)(2,1)}, u32[]{:S(2)}, u32[]{:S(2)}) collective-permute-start(bf16[512,3584]{1,0:T(8,128)(2,1)} %bitcast.14.refs_13_.refs_19_), channel_id=1, source_target_pairs={{144,24},{145,25},{146,26},{147,27},{148,28},{149,29},{150,30},{15... | collective-permute-start | bytes 11010056 | tf_op jit(solution)/shard_map/ppermute | solution.py:40
  86.0 9.7 %collective-permute-start.9 = (bf16[2,16,3584]{2,1,0:T(8,128)(2,1)S(1)}, bf16[2,16,3584]{2,1,0:T(8,128)(2,1)S(1)}, u32[]{:S(2)}, u32[]{:S(2)}) collective-permute-start(bf16[2,16,3584]{2,1,0:T(8,128)(2,1)S(1)} %get-tuple-element.27), channel_id=1, source_target_pairs={{0,1},{1,2},{2,3},{3,4},{4,5},{5,6},{6,7},{7,0},{8,9},{9,10},{10,1... | collective-permute-start | bytes 688136 | tf_op jit(solution)/shard_map/ppermute | solution.py:21
  87.0 12.5 %collective-permute-start.14 = (bf16[4,16,3584]{2,1,0:T(8,128)(2,1)S(1)}, bf16[4,16,3584]{2,1,0:T(8,128)(2,1)S(1)}, u32[]{:S(2)}, u32[]{:S(2)}) collective-permute-start(bf16[4,16,3584]{2,1,0:T(8,128)(2,1)S(1)} %pad_maximum_fusion.2), channel_id=1, source_target_pairs={{0,7},{1,0},{2,1},{3,2},{4,3},{5,4},{6,5},{7,6},{8,15},{9,8},{10,9... | collective-permute-start | bytes 1376264 | tf_op jit(solution)/shard_map/ppermute | solution.py:25
  95.8 12.9 %collective-permute-start.10 = (bf16[4,16,3584]{2,1,0:T(8,128)(2,1)S(1)}, bf16[4,16,3584]{2,1,0:T(8,128)(2,1)S(1)}, u32[]{:S(2)}, u32[]{:S(2)}) collective-permute-start(bf16[4,16,3584]{2,1,0:T(8,128)(2,1)S(1)} %pad_maximum_fusion.1), channel_id=1, source_target_pairs={{0,1},{1,2},{2,3},{3,4},{4,5},{5,6},{6,7},{7,0},{8,9},{9,10},{10,1... | collective-permute-start | bytes 1376264 | tf_op jit(solution)/shard_map/ppermute | solution.py:21
  99.6 12.7 %collective-permute-start.15 = (bf16[4,16,3584]{2,1,0:T(8,128)(2,1)S(1)}, bf16[4,16,3584]{2,1,0:T(8,128)(2,1)S(1)}, u32[]{:S(2)}, u32[]{:S(2)}) collective-permute-start(bf16[4,16,3584]{2,1,0:T(8,128)(2,1)S(1)} %add_convert_fusion.2), channel_id=1, source_target_pairs={{0,7},{1,0},{2,1},{3,2},{4,3},{5,4},{6,5},{7,6},{8,15},{9,8},{10,9... | collective-permute-start | bytes 1376264 | tf_op jit(solution)/shard_map/ppermute | solution.py:25
  108.8 13.6 %collective-permute-start.11 = (bf16[4,16,3584]{2,1,0:T(8,128)(2,1)S(1)}, bf16[4,16,3584]{2,1,0:T(8,128)(2,1)S(1)}, u32[]{:S(2)}, u32[]{:S(2)}) collective-permute-start(bf16[4,16,3584]{2,1,0:T(8,128)(2,1)S(1)} %add_convert_fusion.4), channel_id=1, source_target_pairs={{0,1},{1,2},{2,3},{3,4},{4,5},{5,6},{6,7},{7,0},{8,9},{9,10},{10,1... | collective-permute-start | bytes 1376264 | tf_op jit(solution)/shard_map/ppermute | solution.py:21
  112.3 106.0 %copy-start.16 = (bf16[2,1,16,3584]{3,2,1,0:T(8,128)(2,1)S(1)}, bf16[2,1,16,3584]{3,2,1,0:T(8,128)(2,1)}, u32[]{:S(2)}) copy-start(bf16[2,1,16,3584]{3,2,1,0:T(8,128)(2,1)} %copy-done.15) | copy-start | bytes 688132
  112.4 106.1 %copy-start.18 = (bf16[2,1,16,3584]{3,2,1,0:T(8,128)(2,1)S(1)}, bf16[2,1,16,3584]{3,2,1,0:T(8,128)(2,1)}, u32[]{:S(2)}) copy-start(bf16[2,1,16,3584]{3,2,1,0:T(8,128)(2,1)} %copy-done.17) | copy-start | bytes 688132
  112.5 10.1 %collective-permute-start.16 = (bf16[4,16,3584]{2,1,0:T(8,128)(2,1)S(1)}, bf16[4,16,3584]{2,1,0:T(8,128)(2,1)S(1)}, u32[]{:S(2)}, u32[]{:S(2)}) collective-permute-start(bf16[4,16,3584]{2,1,0:T(8,128)(2,1)S(1)} %add_convert_fusion.1), channel_id=1, source_target_pairs={{0,7},{1,0},{2,1},{3,2},{4,3},{5,4},{6,5},{7,6},{8,15},{9,8},{10,9... | collective-permute-start | bytes 1376264 | tf_op jit(solution)/shard_map/ppermute | solution.py:25
  122.5 9.8 %collective-permute-start.12 = (bf16[4,16,3584]{2,1,0:T(8,128)(2,1)S(1)}, bf16[4,16,3584]{2,1,0:T(8,128)(2,1)S(1)}, u32[]{:S(2)}, u32[]{:S(2)}) collective-permute-start(bf16[4,16,3584]{2,1,0:T(8,128)(2,1)S(1)} %add_convert_fusion.3), channel_id=1, source_target_pairs={{0,1},{1,2},{2,3},{3,4},{4,5},{5,6},{6,7},{7,0},{8,9},{9,10},{10,1... | collective-permute-start | bytes 1376264 | tf_op jit(solution)/shard_map/ppermute | solution.py:21
  133.1 39.8 %collective-permute-start.17 = (bf16[2,16,3584]{2,1,0:T(8,128)(2,1)}, bf16[2,16,3584]{2,1,0:T(8,128)(2,1)}, u32[]{:S(2)}, u32[]{:S(2)}) collective-permute-start(bf16[2,16,3584]{2,1,0:T(8,128)(2,1)} %slice.95), channel_id=1, source_target_pairs={{0,136},{1,137},{2,138},{3,139},{4,140},{5,141},{6,142},{7,143},{8... | collective-permute-start | bytes 688136 | tf_op jit(solution)/shard_map/ppermute | solution.py:34
  143.2 37.0 %collective-permute-start.19 = (f32[40,3584]{1,0:T(8,128)S(1)}, f32[40,3584]{1,0:T(8,128)}, u32[]{:S(2)}, u32[]{:S(2)}) collective-permute-start(f32[40,3584]{1,0:T(8,128)S(1)} %concatenate.15.refs_9_), channel_id=1, source_target_pairs={{128,8},{129,9},{130,10},{131,11},{132,12},{133,13},{134,14},{135,... | collective-permute-start | bytes 1720328 | tf_op jit(solution)/shard_map/ppermute | solution.py:40
  144.5 71.2 %collective-permute-start.28 = (bf16[3584,256]{1,0:T(8,128)(2,1)S(1)}, bf16[3584,256]{1,0:T(8,128)(2,1)}, u32[]{:S(2)}, u32[]{:S(2)}) collective-permute-start(bf16[3584,256]{1,0:T(8,128)(2,1)S(1)} %bitcast.51), channel_id=1, source_target_pairs={{128,8},{129,9},{130,10},{131,11},{132,12},{133,13},{134,14},{135,... | collective-permute-start | bytes 5505032 | tf_op jit(solution)/shard_map/ppermute | solution.py:40
  167.9 49.2 %collective-permute-start.30 = (bf16[3584,256]{1,0:T(8,128)(2,1)}, bf16[3584,256]{1,0:T(8,128)(2,1)}, u32[]{:S(2)}, u32[]{:S(2)}) collective-permute-start(bf16[3584,256]{1,0:T(8,128)(2,1)} %bitcast.54), channel_id=1, source_target_pairs={{144,24},{145,25},{146,26},{147,27},{148,28},{149,29},{150,30},{15... | collective-permute-start | bytes 5505032 | tf_op jit(solution)/shard_map/ppermute | solution.py:40
  169.8 102.4 %collective-permute-start.33 = (bf16[3584,512]{1,0:T(8,128)(2,1)}, bf16[3584,512]{1,0:T(8,128)(2,1)}, u32[]{:S(2)}, u32[]{:S(2)}) collective-permute-start(bf16[3584,512]{1,0:T(8,128)(2,1)} %collective-permute-done.32.refs_17_), channel_id=1, source_target_pairs={{0,16},{32,48},{64,80},{96,112},{1,17},{33,49},{65,81},{97,113},{2... | collective-permute-start | bytes 11010056 | tf_op jit(solution)/shard_map/ppermute | solution.py:45
  173.0 99.2 %collective-permute-start.35 = (bf16[512,3584]{1,0:T(8,128)(2,1)}, bf16[512,3584]{1,0:T(8,128)(2,1)}, u32[]{:S(2)}, u32[]{:S(2)}) collective-permute-start(bf16[512,3584]{1,0:T(8,128)(2,1)} %collective-permute-done.34.refs_20_), channel_id=1, source_target_pairs={{16,0},{48,32},{80,64},{112,96},{17,1},{49,33},{81,65},{113,97},{1... | collective-permute-start | bytes 11010056 | tf_op jit(solution)/shard_map/ppermute | solution.py:45
  180.2 38.2 %collective-permute-start.18 = (bf16[2,16,3584]{2,1,0:T(8,128)(2,1)S(1)}, bf16[2,16,3584]{2,1,0:T(8,128)(2,1)S(1)}, u32[]{:S(2)}, u32[]{:S(2)}) collective-permute-start(bf16[2,16,3584]{2,1,0:T(8,128)(2,1)S(1)} %slice_select_fusion), channel_id=1, source_target_pairs={{0,8},{1,9},{2,10},{3,11},{4,12},{5,13},{6,14},{7,15},{8,0},{9,1},... | collective-permute-start | bytes 688136 | tf_op jit(solution)/shard_map/ppermute | solution.py:29
  215.7 49.2 %collective-permute-start.29 = (bf16[3584,256]{1,0:T(8,128)(2,1)}, bf16[3584,256]{1,0:T(8,128)(2,1)S(1)}, u32[]{:S(2)}, u32[]{:S(2)}) collective-permute-start(bf16[3584,256]{1,0:T(8,128)(2,1)} %collective-permute-done.28.refs_11_), channel_id=1, source_target_pairs={{0,16},{32,48},{64,80},{96,112},{1,17},{33,49},{65,81},{97,113},{2... | collective-permute-start | bytes 5505032 | tf_op jit(solution)/shard_map/ppermute | solution.py:45
  217.1 52.5 %collective-permute-start.31 = (bf16[3584,256]{1,0:T(8,128)(2,1)}, bf16[3584,256]{1,0:T(8,128)(2,1)}, u32[]{:S(2)}, u32[]{:S(2)}) collective-permute-start(bf16[3584,256]{1,0:T(8,128)(2,1)} %collective-permute-done.30.refs_14_), channel_id=1, source_target_pairs={{16,0},{48,32},{80,64},{112,96},{17,1},{49,33},{81,65},{113,97},{1... | collective-permute-start | bytes 5505032 | tf_op jit(solution)/shard_map/ppermute | solution.py:45
  218.8 8.3 %collective-permute-start.23 = (bf16[2,16,3584]{2,1,0:T(8,128)(2,1)S(1)}, bf16[2,16,3584]{2,1,0:T(8,128)(2,1)S(1)}, u32[]{:S(2)}, u32[]{:S(2)}) collective-permute-start(bf16[2,16,3584]{2,1,0:T(8,128)(2,1)S(1)} %fusion.4.refs_0_), channel_id=1, source_target_pairs={{0,1},{1,2},{2,3},{3,4},{4,5},{5,6},{6,7},{7,0},{8,9},{9,10},{10,1... | collective-permute-start | bytes 688136 | tf_op jit(solution)/shard_map/ppermute | solution.py:21
  227.1 8.2 %collective-permute-start.20 = (bf16[2,16,3584]{2,1,0:T(8,128)(2,1)S(1)}, bf16[2,16,3584]{2,1,0:T(8,128)(2,1)S(1)}, u32[]{:S(2)}, u32[]{:S(2)}) collective-permute-start(bf16[2,16,3584]{2,1,0:T(8,128)(2,1)S(1)} %fusion.4.refs_0_), channel_id=1, source_target_pairs={{0,7},{1,0},{2,1},{3,2},{4,3},{5,4},{6,5},{7,6},{8,15},{9,8},{10,9... | collective-permute-start | bytes 688136 | tf_op jit(solution)/shard_map/ppermute | solution.py:25
  235.3 8.8 %collective-permute-start.24 = (bf16[2,16,3584]{2,1,0:T(8,128)(2,1)S(1)}, bf16[2,16,3584]{2,1,0:T(8,128)(2,1)S(1)}, u32[]{:S(2)}, u32[]{:S(2)}) collective-permute-start(bf16[2,16,3584]{2,1,0:T(8,128)(2,1)S(1)} %collective-permute-done.23.refs_6_), channel_id=1, source_target_pairs={{0,1},{1,2},{2,3},{3,4},{4,5},{5,6},{6,7},{7,0},{8,9},{9,10},{10,1... | collective-permute-start | bytes 688136 | tf_op jit(solution)/shard_map/ppermute | solution.py:21
  244.2 6.8 %collective-permute-start.21 = (bf16[2,16,3584]{2,1,0:T(8,128)(2,1)S(1)}, bf16[2,16,3584]{2,1,0:T(8,128)(2,1)S(1)}, u32[]{:S(2)}, u32[]{:S(2)}) collective-permute-start(bf16[2,16,3584]{2,1,0:T(8,128)(2,1)S(1)} %collective-permute-done.20.refs_1_), channel_id=1, source_target_pairs={{0,7},{1,0},{2,1},{3,2},{4,3},{5,4},{6,5},{7,6},{8,15},{9,8},{10,9... | collective-permute-start | bytes 688136 | tf_op jit(solution)/shard_map/ppermute | solution.py:25
  251.0 7.2 %collective-permute-start.25 = (bf16[2,16,3584]{2,1,0:T(8,128)(2,1)S(1)}, bf16[2,16,3584]{2,1,0:T(8,128)(2,1)S(1)}, u32[]{:S(2)}, u32[]{:S(2)}) collective-permute-start(bf16[2,16,3584]{2,1,0:T(8,128)(2,1)S(1)} %collective-permute-done.24.refs_5_), channel_id=1, source_target_pairs={{0,1},{1,2},{2,3},{3,4},{4,5},{5,6},{6,7},{7,0},{8,9},{9,10},{10,1... | collective-permute-start | bytes 688136 | tf_op jit(solution)/shard_map/ppermute | solution.py:21
  258.2 6.0 %collective-permute-start.22 = (bf16[2,16,3584]{2,1,0:T(8,128)(2,1)S(1)}, bf16[2,16,3584]{2,1,0:T(8,128)(2,1)S(1)}, u32[]{:S(2)}, u32[]{:S(2)}) collective-permute-start(bf16[2,16,3584]{2,1,0:T(8,128)(2,1)S(1)} %collective-permute-done.21.refs_2_), channel_id=1, source_target_pairs={{0,7},{1,0},{2,1},{3,2},{4,3},{5,4},{6,5},{7,6},{8,15},{9,8},{10,9... | collective-permute-start | bytes 688136 | tf_op jit(solution)/shard_map/ppermute | solution.py:25
  264.2 6.2 %collective-permute-start.26 = (bf16[1,16,3584]{2,1,0:T(8,128)(2,1)}, bf16[1,16,3584]{2,1,0:T(8,128)(2,1)S(1)}, u32[]{:S(2)}, u32[]{:S(2)}) collective-permute-start(bf16[1,16,3584]{2,1,0:T(8,128)(2,1)} %slice.99), channel_id=1, source_target_pairs={{0,1},{1,2},{2,3},{3,4},{4,5},{5,6},{6,7},{7,0},{8,9},{9,10},{10,1... | collective-permute-start | bytes 344072 | tf_op jit(solution)/shard_map/ppermute | solution.py:21
  266.1 6.1 %collective-permute-start.27 = (bf16[1,16,3584]{2,1,0:T(8,128)(2,1)}, bf16[1,16,3584]{2,1,0:T(8,128)(2,1)S(1)}, u32[]{:S(2)}, u32[]{:S(2)}) collective-permute-start(bf16[1,16,3584]{2,1,0:T(8,128)(2,1)} %slice.100), channel_id=1, source_target_pairs={{0,7},{1,0},{2,1},{3,2},{4,3},{5,4},{6,5},{7,6},{8,15},{9,8},{10,9... | collective-permute-start | bytes 344072 | tf_op jit(solution)/shard_map/ppermute | solution.py:25
  288.5 6.8 %collective-permute-start.40 = (bf16[1,16,3584]{2,1,0:T(8,128)(2,1)S(1)}, bf16[1,16,3584]{2,1,0:T(8,128)(2,1)S(1)}, u32[]{:S(2)}, u32[]{:S(2)}) collective-permute-start(bf16[1,16,3584]{2,1,0:T(8,128)(2,1)S(1)} %get-tuple-element.40), channel_id=1, source_target_pairs={{0,7},{1,0},{2,1},{3,2},{4,3},{5,4},{6,5},{7,6},{8,15},{9,8},{10,9... | collective-permute-start | bytes 344072 | tf_op jit(solution)/shard_map/ppermute | solution.py:25
  292.1 7.0 %collective-permute-start.36 = (bf16[1,16,3584]{2,1,0:T(8,128)(2,1)S(1)}, bf16[1,16,3584]{2,1,0:T(8,128)(2,1)S(1)}, u32[]{:S(2)}, u32[]{:S(2)}) collective-permute-start(bf16[1,16,3584]{2,1,0:T(8,128)(2,1)S(1)} %get-tuple-element.36), channel_id=1, source_target_pairs={{0,1},{1,2},{2,3},{3,4},{4,5},{5,6},{6,7},{7,0},{8,9},{9,10},{10,1... | collective-permute-start | bytes 344072 | tf_op jit(solution)/shard_map/ppermute | solution.py:21
  295.3 8.4 %collective-permute-start.41 = (bf16[2,16,3584]{2,1,0:T(8,128)(2,1)S(1)}, bf16[2,16,3584]{2,1,0:T(8,128)(2,1)S(1)}, u32[]{:S(2)}, u32[]{:S(2)}) collective-permute-start(bf16[2,16,3584]{2,1,0:T(8,128)(2,1)S(1)} %pad_maximum_fusion.4), channel_id=1, source_target_pairs={{0,7},{1,0},{2,1},{3,2},{4,3},{5,4},{6,5},{7,6},{8,15},{9,8},{10,9... | collective-permute-start | bytes 688136 | tf_op jit(solution)/shard_map/ppermute | solution.py:25
  299.1 8.4 %collective-permute-start.37 = (bf16[2,16,3584]{2,1,0:T(8,128)(2,1)S(1)}, bf16[2,16,3584]{2,1,0:T(8,128)(2,1)S(1)}, u32[]{:S(2)}, u32[]{:S(2)}) collective-permute-start(bf16[2,16,3584]{2,1,0:T(8,128)(2,1)S(1)} %pad_maximum_fusion.3), channel_id=1, source_target_pairs={{0,1},{1,2},{2,3},{3,4},{4,5},{5,6},{6,7},{7,0},{8,9},{9,10},{10,1... | collective-permute-start | bytes 688136 | tf_op jit(solution)/shard_map/ppermute | solution.py:21
  303.8 7.5 %collective-permute-start.42 = (bf16[2,16,3584]{2,1,0:T(8,128)(2,1)S(1)}, bf16[2,16,3584]{2,1,0:T(8,128)(2,1)S(1)}, u32[]{:S(2)}, u32[]{:S(2)}) collective-permute-start(bf16[2,16,3584]{2,1,0:T(8,128)(2,1)S(1)} %add_convert_fusion.6), channel_id=1, source_target_pairs={{0,7},{1,0},{2,1},{3,2},{4,3},{5,4},{6,5},{7,6},{8,15},{9,8},{10,9... | collective-permute-start | bytes 688136 | tf_op jit(solution)/shard_map/ppermute | solution.py:25
  307.6 7.5 %collective-permute-start.38 = (bf16[2,16,3584]{2,1,0:T(8,128)(2,1)S(1)}, bf16[2,16,3584]{2,1,0:T(8,128)(2,1)S(1)}, u32[]{:S(2)}, u32[]{:S(2)}) collective-permute-start(bf16[2,16,3584]{2,1,0:T(8,128)(2,1)S(1)} %add_convert_fusion.8), channel_id=1, source_target_pairs={{0,1},{1,2},{2,3},{3,4},{4,5},{5,6},{6,7},{7,0},{8,9},{9,10},{10,1... | collective-permute-start | bytes 688136 | tf_op jit(solution)/shard_map/ppermute | solution.py:21
  311.4 7.3 %collective-permute-start.43 = (bf16[2,16,3584]{2,1,0:T(8,128)(2,1)S(1)}, bf16[2,16,3584]{2,1,0:T(8,128)(2,1)S(1)}, u32[]{:S(2)}, u32[]{:S(2)}) collective-permute-start(bf16[2,16,3584]{2,1,0:T(8,128)(2,1)S(1)} %add_convert_fusion.5), channel_id=1, source_target_pairs={{0,7},{1,0},{2,1},{3,2},{4,3},{5,4},{6,5},{7,6},{8,15},{9,8},{10,9... | collective-permute-start | bytes 688136 | tf_op jit(solution)/shard_map/ppermute | solution.py:25
  315.2 7.3 %collective-permute-start.39 = (bf16[2,16,3584]{2,1,0:T(8,128)(2,1)S(1)}, bf16[2,16,3584]{2,1,0:T(8,128)(2,1)S(1)}, u32[]{:S(2)}, u32[]{:S(2)}) collective-permute-start(bf16[2,16,3584]{2,1,0:T(8,128)(2,1)S(1)} %add_convert_fusion.7), channel_id=1, source_target_pairs={{0,1},{1,2},{2,3},{3,4},{4,5},{5,6},{6,7},{7,0},{8,9},{9,10},{10,1... | collective-permute-start | bytes 688136 | tf_op jit(solution)/shard_map/ppermute | solution.py:21
  322.7 4.9 %collective-permute-start.44 = (bf16[16,3584]{1,0:T(8,128)(2,1)S(1)}, bf16[16,3584]{1,0:T(8,128)(2,1)S(1)}, u32[]{:S(2)}, u32[]{:S(2)}) collective-permute-start(bf16[16,3584]{1,0:T(8,128)(2,1)S(1)} %fusion.12), channel_id=1, source_target_pairs={{0,8},{1,9},{2,10},{3,11},{4,12},{5,13},{6,14},{7,15},{8,0},{9,1},... | collective-permute-start | bytes 344072 | tf_op jit(solution)/shard_map/ppermute | solution.py:29
  (23 other events, 313.6 us)
